TPU v7x, 256 devices: a whole 4x4x8 slice. The times are simulated.
256 devices in a mesh: row: 16 (over x, y), col: 16 (over z, core).
Axes of the slice: x: 4, y: 4, z: 8, core: 2. Of those that a mesh axis runs over, the one named last changes fastest.
Arguments:
- entities: bfloat16 [65536, 512], P(('row', 'col')), may hold values from -6 to 6
- entity_bias: bfloat16 [8, 65536], P(None, ('row', 'col')), may hold values from -2 to 250
- w_query: bfloat16 [512, 512], replicated, may hold values from -0.5 to 0.5
- w_key: bfloat16 [512, 512], replicated, may hold values from -0.5 to 0.5
- w_value: bfloat16 [512, 512], replicated, may hold values from -0.25 to 0.25
- w_out: bfloat16 [512, 512], replicated, may hold values from -0.25 to 0.25
- tile_index: int32 [512, 16, 6], P('row', 'col'), may hold values from 0 to 31, as said below
- tile_count: int32 [512, 16], P('row', 'col'), may hold values from 1 to 6, as said below
Outputs:
- updated: float32 [65536, 512], P(('row', 'col'))
Inputs may be any that keep to these rules, and one draw needn't show every extreme that they name: `tile_index`: each list holds 6 distinct tile numbers of its source group; slots at or after the count are ignored. `tile_count`: every destination block of 32 tiles has, in each source group, one list with 6 live slots and one with a single live slot.
All inputs are finite; a program needn't handle non-finite values.
Results may differ from a plain program's by a relative error of at most 0.013.
Values may be sent and summed in bfloat16 or wider, within the bound.
No kernel may reach another device: no remote copies, remote signals or barrier semaphores. Data moves between devices by JAX's collectives and lax.ppermute only.
A program may use at most 128 MiB of HBM per device.

v0:
```python
import math

import jax
import jax.numpy as jnp
from jax import lax
from jax.sharding import PartitionSpec as P

TILE = 128
MAXT = 6


def rms_norm(activations):
    values_f = activations.astype(jnp.float32)
    scale_inv = lax.rsqrt(jnp.mean(values_f * values_f, axis=-1, keepdims=True) + 1e-06)
    return (values_f * scale_inv).astype(jnp.bfloat16)


def project(normed, weights):
    return jnp.dot(normed, weights, preferred_element_type=jnp.float32).astype(jnp.bfloat16)


def body(entities, entity_bias, w_query, w_key, w_value, w_out, tile_index, tile_count):
    own_rows, model_width = entities.shape
    head_count = entity_bias.shape[0]
    head_size = model_width // head_count
    normed = rms_norm(entities)
    query_rows = project(normed, w_query)
    block_queries = lax.all_gather(query_rows, "col", axis=0, tiled=True)
    key_rows = project(normed, w_key)
    value_rows = project(normed, w_value)
    source_keys, source_values, source_bias = (
        lax.all_gather(key_rows, "row", axis=0, tiled=True),
        lax.all_gather(value_rows, "row", axis=0, tiled=True),
        lax.all_gather(entity_bias, "row", axis=1, tiled=True),
    )
    src_tiles = source_keys.shape[0] // TILE
    dest_tiles = block_queries.shape[0] // TILE
    tile_group = math.gcd(dest_tiles, max(1, 512 // TILE))
    batches = dest_tiles // tile_group
    span = MAXT * TILE
    key_tiles = source_keys.reshape(src_tiles, TILE, head_count, head_size)
    value_tiles = source_values.reshape(src_tiles, TILE, head_count, head_size)
    bias_tiles = source_bias.reshape(head_count, src_tiles, TILE)
    query_groups = block_queries.reshape(batches, tile_group, TILE, head_count, head_size)
    id_groups = tile_index.reshape(batches, tile_group, MAXT)
    count_groups = tile_count.reshape(batches, tile_group)
    score_scale = 1.0 / math.sqrt(head_size)

    def attend(inputs):
        query_block, tile_ids, counts = inputs
        near_keys = key_tiles[tile_ids].reshape(tile_group, span, head_count, head_size)
        near_values = value_tiles[tile_ids].reshape(tile_group, span, head_count, head_size)
        near_bias = jnp.transpose(
            bias_tiles[:, tile_ids].reshape(head_count, tile_group, span), (1, 0, 2)
        ).astype(jnp.float32)
        scores = (
            jnp.einsum(
                "gqhd,gkhd->ghqk", query_block, near_keys, preferred_element_type=jnp.float32
            )
            * score_scale
        )
        scores = scores + near_bias[:, :, None, :]
        slot_ids = lax.broadcasted_iota(jnp.int32, (tile_group, MAXT, TILE), 1)
        live_slots = (slot_ids < counts[:, None, None]).reshape(tile_group, 1, 1, span)
        group_peak = jnp.max(jnp.where(live_slots, scores, -1e30), axis=-1)
        weight = jnp.where(live_slots, jnp.exp(scores - group_peak[..., None]), 0.0)
        group_total = jnp.sum(weight, axis=-1)
        group_num = jnp.einsum(
            "ghqk,gkhd->gqhd",
            weight.astype(jnp.bfloat16),
            near_values,
            preferred_element_type=jnp.float32,
        )
        return (group_num, group_total, group_peak)

    group_num, group_total, group_peak = lax.map(attend, (query_groups, id_groups, count_groups))
    block_rows = dest_tiles * TILE
    group_num = group_num.reshape(block_rows, model_width)
    group_total = jnp.transpose(group_total, (2, 0, 1, 3)).reshape(head_count, block_rows)
    group_peak = jnp.transpose(group_peak, (2, 0, 1, 3)).reshape(head_count, block_rows)
    row_peak = lax.pmax(group_peak.astype(jnp.bfloat16), "col").astype(group_peak.dtype)
    factor = jnp.exp(group_peak - row_peak)
    scaled = (
        group_num.reshape(block_rows, head_count, head_size) * jnp.transpose(factor)[:, :, None]
    ).reshape(block_rows, model_width)
    numerator, denominator = (
        lax.psum_scatter(
            scaled.astype(jnp.bfloat16), "col", scatter_dimension=0, tiled=True
        ).astype(jnp.float32),
        lax.psum_scatter(
            (group_total * factor).astype(jnp.bfloat16), "col", scatter_dimension=1, tiled=True
        ).astype(jnp.float32),
    )
    attended = (
        (
            numerator.reshape(own_rows, head_count, head_size)
            / jnp.transpose(denominator)[:, :, None]
        )
        .reshape(own_rows, model_width)
        .astype(jnp.bfloat16)
    )
    return entities.astype(jnp.float32) + jnp.dot(
        attended, w_out, preferred_element_type=jnp.float32
    )


def solution(mesh):
    placed = (
        P(("row", "col"), None),
        P(None, ("row", "col")),
        P(),
        P(),
        P(),
        P(),
        P("row", "col", None),
        P("row", "col"),
    )
    return jax.shard_map(
        body, mesh=mesh, in_specs=placed, out_specs=P(("row", "col"), None), check_vma=False
    )
```

profile of v0, /device:TPU:56, one launch (start us, length us, event | category | flops | bytes accessed | tf_op | source)
XLA Modules:
  0.0 737.2 jit_solution(10157258740435518324)
XLA Ops:
  17.0 23.3 %all_gather.15 = bf16[8,4096]{1,0:T(8,128)(2,1)S(1)} all-gather(bf16[8,256]{1,0:T(8,128)(2,1)} %param.11), channel_id=1, replica_groups=mesh['row'=16,'col'=16] {'row'}, dimensions={1}, use_global_device_ids=true | all-gather | bytes 69632 | tf_op jit(solution)/shard_map/all_gather | solution.py:34
  40.3 13.7 %all-gather.6.cloned.1.call-done = bf16[4096,512]{1,0:T(8,128)(2,1)} async-done(((bf16[256,512]{1,0:T(8,128)(2,1)}), bf16[4096,512]{1,0:T(8,128)(2,1)}) %all-gather.6.cloned.1.call-update) | async-done | bytes 4194320 | tf_op jit(solution)/shard_map/all_gather | solution.py:28
  54.0 11.2 %reshape.136 = bf16[8,4,128,8,64]{4,3,2,1,0:T(8,128)(2,1)} reshape(bf16[4096,512]{1,0:T(8,128)(2,1)} %all-gather.6.cloned.1.call-done) | data formatting | bytes 8388608 | tf_op jit(solution)/shard_map/reshape | solution.py:44
  65.2 9.1 %copy.21 = bf16[8,4,128,8,64]{2,4,3,1,0:T(8,128)(2,1)} copy(bf16[8,4,128,8,64]{4,3,2,1,0:T(8,128)(2,1)} %reshape.136) | data formatting | bytes 8388608 | tf_op jit(solution)/shard_map/while | solution.py:76
  74.3 37.5 %all-gather.4.cloned.1.call-done = bf16[4096,512]{1,0:T(8,128)(2,1)} async-done(((bf16[256,512]{1,0:T(8,128)(2,1)}), bf16[4096,512]{1,0:T(8,128)(2,1)}) %all-gather.4.cloned.1.call-update) | async-done | bytes 4194320 | tf_op jit(solution)/shard_map/all_gather | solution.py:33
  111.8 11.2 %reshape.135 = bf16[32,128,8,64]{3,2,1,0:T(8,128)(2,1)} reshape(bf16[4096,512]{1,0:T(8,128)(2,1)} %all-gather.4.cloned.1.call-done) | data formatting | bytes 8388608 | tf_op jit(solution)/shard_map/reshape | solution.py:42
  123.0 47.6 %all-gather.8.cloned.1.call-done = bf16[4096,512]{1,0:T(8,128)(2,1)} async-done(((bf16[256,512]{1,0:T(8,128)(2,1)}), bf16[4096,512]{1,0:T(8,128)(2,1)}) %all-gather.8.cloned.1.call-update) | async-done | bytes 4194320 | tf_op jit(solution)/shard_map/all_gather | solution.py:32
  170.6 11.2 %reshape.137 = bf16[32,128,8,64]{3,2,1,0:T(8,128)(2,1)} reshape(bf16[4096,512]{1,0:T(8,128)(2,1)} %all-gather.8.cloned.1.call-done) | data formatting | bytes 8388608 | tf_op jit(solution)/shard_map/reshape | solution.py:41
  181.8 329.7 %while.14 = (s32[]{:T(128)}, f32[8,4,128,8,64]{2,1,0,4,3:T(4,128)}, f32[8,4,8,128]{3,2,1,0:T(8,128)S(1)}, f32[8,4,8,128]{3,2,1,0:T(8,128)S(1)}, s32[8,4,6]{2,1,0...) while((s32[]{:T(128)}, f32[8,4,128,8,64]{2,1,0,4,3:T(4,128)}, ...), condition=%wide.region_4.5_spmd, body=%wide.region_1.4_spmd.sunk | while | flops 849367104 | bytes 114466752 | solution.py:76
  212.5 8.7 %fusion.43 = f32[1,4,128,8,64]{2,4,3,1,0:T(8,128)S(1)} fusion(f32[4,8,128,768]{3,2,1,0:T(8,128)} %copy-done.2, f32[4,8,128]{2,1,0:T(8,128)S(1)} %get-tuple-element.174, f32[4,8,768]{2,1,0:T(8,128)S(1)} %convert_bitcast_fusion.3, pred[4,768]{1,0:T(4,128)(4,1)S(1)} %broadcast_compare_fusion.2, bf16[4,768,8,64]{3,2,1,0:T(8,128)(2,1)} %bitcast.80), kind=kOutput, calls=%fused_computation.16.clone.1 | convolution fusion | flops 418381824 | bytes 16894976 | tf_op jit(solution)/shard_map/while/body/eval_jaxpr/ghqk,gkhd->gqhd/dot_general | solution.py:68
  223.6 7.8 %gather_fusion.1 = bf16[24,128,8,64]{3,2,1,0:T(8,128)(2,1)} fusion(bf16[32,128,8,64]{3,2,1,0:T(8,128)(2,1)} %get-tuple-element.207, s32[1024]{0:T(1024)S(1)} %pad_clamp_fusion.2), kind=kCustom, calls=%fused_computation.1.clone.1 | custom fusion | bytes 6291552 | tf_op jit(solution)/shard_map/while/body/eval_jaxpr/gather | solution.py:51
  253.7 8.7 %fusion.43 = f32[1,4,128,8,64]{2,4,3,1,0:T(8,128)S(1)} fusion(f32[4,8,128,768]{3,2,1,0:T(8,128)} %copy-done.2, f32[4,8,128]{2,1,0:T(8,128)S(1)} %get-tuple-element.174, f32[4,8,768]{2,1,0:T(8,128)S(1)} %convert_bitcast_fusion.3, pred[4,768]{1,0:T(4,128)(4,1)S(1)} %broadcast_compare_fusion.2, bf16[4,768,8,64]{3,2,1,0:T(8,128)(2,1)} %bitcast.80), kind=kOutput, calls=%fused_computation.16.clone.1 | convolution fusion | flops 418381824 | bytes 16894976 | tf_op jit(solution)/shard_map/while/body/eval_jaxpr/ghqk,gkhd->gqhd/dot_general | solution.py:68
  294.9 8.7 %fusion.43 = f32[1,4,128,8,64]{2,4,3,1,0:T(8,128)S(1)} fusion(f32[4,8,128,768]{3,2,1,0:T(8,128)} %copy-done.2, f32[4,8,128]{2,1,0:T(8,128)S(1)} %get-tuple-element.174, f32[4,8,768]{2,1,0:T(8,128)S(1)} %convert_bitcast_fusion.3, pred[4,768]{1,0:T(4,128)(4,1)S(1)} %broadcast_compare_fusion.2, bf16[4,768,8,64]{3,2,1,0:T(8,128)(2,1)} %bitcast.80), kind=kOutput, calls=%fused_computation.16.clone.1 | convolution fusion | flops 418381824 | bytes 16894976 | tf_op jit(solution)/shard_map/while/body/eval_jaxpr/ghqk,gkhd->gqhd/dot_general | solution.py:68
  336.1 8.7 %fusion.43 = f32[1,4,128,8,64]{2,4,3,1,0:T(8,128)S(1)} fusion(f32[4,8,128,768]{3,2,1,0:T(8,128)} %copy-done.2, f32[4,8,128]{2,1,0:T(8,128)S(1)} %get-tuple-element.174, f32[4,8,768]{2,1,0:T(8,128)S(1)} %convert_bitcast_fusion.3, pred[4,768]{1,0:T(4,128)(4,1)S(1)} %broadcast_compare_fusion.2, bf16[4,768,8,64]{3,2,1,0:T(8,128)(2,1)} %bitcast.80), kind=kOutput, calls=%fused_computation.16.clone.1 | convolution fusion | flops 418381824 | bytes 16894976 | tf_op jit(solution)/shard_map/while/body/eval_jaxpr/ghqk,gkhd->gqhd/dot_general | solution.py:68
  347.3 7.8 %gather_fusion.1 = bf16[24,128,8,64]{3,2,1,0:T(8,128)(2,1)} fusion(bf16[32,128,8,64]{3,2,1,0:T(8,128)(2,1)} %get-tuple-element.207, s32[1024]{0:T(1024)S(1)} %pad_clamp_fusion.2), kind=kCustom, calls=%fused_computation.1.clone.1 | custom fusion | bytes 6291552 | tf_op jit(solution)/shard_map/while/body/eval_jaxpr/gather | solution.py:51
  377.4 8.7 %fusion.43 = f32[1,4,128,8,64]{2,4,3,1,0:T(8,128)S(1)} fusion(f32[4,8,128,768]{3,2,1,0:T(8,128)} %copy-done.2, f32[4,8,128]{2,1,0:T(8,128)S(1)} %get-tuple-element.174, f32[4,8,768]{2,1,0:T(8,128)S(1)} %convert_bitcast_fusion.3, pred[4,768]{1,0:T(4,128)(4,1)S(1)} %broadcast_compare_fusion.2, bf16[4,768,8,64]{3,2,1,0:T(8,128)(2,1)} %bitcast.80), kind=kOutput, calls=%fused_computation.16.clone.1 | convolution fusion | flops 418381824 | bytes 16894976 | tf_op jit(solution)/shard_map/while/body/eval_jaxpr/ghqk,gkhd->gqhd/dot_general | solution.py:68
  418.6 8.7 %fusion.43 = f32[1,4,128,8,64]{2,4,3,1,0:T(8,128)S(1)} fusion(f32[4,8,128,768]{3,2,1,0:T(8,128)} %copy-done.2, f32[4,8,128]{2,1,0:T(8,128)S(1)} %get-tuple-element.174, f32[4,8,768]{2,1,0:T(8,128)S(1)} %convert_bitcast_fusion.3, pred[4,768]{1,0:T(4,128)(4,1)S(1)} %broadcast_compare_fusion.2, bf16[4,768,8,64]{3,2,1,0:T(8,128)(2,1)} %bitcast.80), kind=kOutput, calls=%fused_computation.16.clone.1 | convolution fusion | flops 418381824 | bytes 16894976 | tf_op jit(solution)/shard_map/while/body/eval_jaxpr/ghqk,gkhd->gqhd/dot_general | solution.py:68
  429.7 7.8 %gather_fusion.1 = bf16[24,128,8,64]{3,2,1,0:T(8,128)(2,1)} fusion(bf16[32,128,8,64]{3,2,1,0:T(8,128)(2,1)} %get-tuple-element.207, s32[1024]{0:T(1024)S(1)} %pad_clamp_fusion.2), kind=kCustom, calls=%fused_computation.1.clone.1 | custom fusion | bytes 6291552 | tf_op jit(solution)/shard_map/while/body/eval_jaxpr/gather | solution.py:51
  459.8 8.7 %fusion.43 = f32[1,4,128,8,64]{2,4,3,1,0:T(8,128)S(1)} fusion(f32[4,8,128,768]{3,2,1,0:T(8,128)} %copy-done.2, f32[4,8,128]{2,1,0:T(8,128)S(1)} %get-tuple-element.174, f32[4,8,768]{2,1,0:T(8,128)S(1)} %convert_bitcast_fusion.3, pred[4,768]{1,0:T(4,128)(4,1)S(1)} %broadcast_compare_fusion.2, bf16[4,768,8,64]{3,2,1,0:T(8,128)(2,1)} %bitcast.80), kind=kOutput, calls=%fused_computation.16.clone.1 | convolution fusion | flops 418381824 | bytes 16894976 | tf_op jit(solution)/shard_map/while/body/eval_jaxpr/ghqk,gkhd->gqhd/dot_general | solution.py:68
  501.0 8.7 %fusion.43 = f32[1,4,128,8,64]{2,4,3,1,0:T(8,128)S(1)} fusion(f32[4,8,128,768]{3,2,1,0:T(8,128)} %copy-done.2, f32[4,8,128]{2,1,0:T(8,128)S(1)} %get-tuple-element.174, f32[4,8,768]{2,1,0:T(8,128)S(1)} %convert_bitcast_fusion.3, pred[4,768]{1,0:T(4,128)(4,1)S(1)} %broadcast_compare_fusion.2, bf16[4,768,8,64]{3,2,1,0:T(8,128)(2,1)} %bitcast.80), kind=kOutput, calls=%fused_computation.16.clone.1 | convolution fusion | flops 418381824 | bytes 16894976 | tf_op jit(solution)/shard_map/while/body/eval_jaxpr/ghqk,gkhd->gqhd/dot_general | solution.py:68
  512.2 97.7 %all-reduce.2.cloned.1.call-done = bf16[8,4096]{1,0:T(8,128)(2,1)} async-done(((bf16[8,4096]{1,0:T(8,128)(2,1)}), bf16[8,4096]{1,0:T(8,128)(2,1)}) %all-reduce.2.cloned.1.call-update) | async-done | bytes 65552 | tf_op jit(solution)/shard_map/pmax | solution.py:81
  611.5 10.3 %reshape_reshape.3 = f32[4096,512]{0,1:T(8,128)} reshape(f32[8,4,128,8,64]{2,1,0,4,3:T(4,128)} %get-tuple-element.59) | data formatting | bytes 16777216 | tf_op jit(solution)/shard_map/reshape;reshape | solution.py:84
  628.4 36.3 %reduce-scatter.5.cloned.1.call-done = bf16[8,256]{1,0:T(8,128)(2,1)} async-done(((bf16[8,4096]{1,0:T(8,128)(2,1)}), bf16[8,256]{1,0:T(8,128)(2,1)}) %reduce-scatter.5.cloned.1.call-update) | async-done | bytes 4112 | tf_op jit(solution)/shard_map/reduce_scatter | solution.py:90
  665.4 62.8 %reduce-scatter.3.cloned.1.call-done = bf16[256,512]{0,1:T(8,128)(2,1)} async-done(((bf16[4096,512]{0,1:T(8,128)(2,1)}), bf16[256,512]{0,1:T(8,128)(2,1)}) %reduce-scatter.3.cloned.1.call-update) | async-done | bytes 262160 | tf_op jit(solution)/shard_map/reduce_scatter | solution.py:87
  (163 shorter events, 258.2 us)
Async XLA Ops:
  6.5 1.2 copy-start
  6.5 47.5 %all-gather.6.cloned.1.call-start = ((), (), s32[]{:S(2)}) async-start(), calls=%async_computation.3 | async-start | bytes 4456448 | tf_op jit(solution)/shard_map/all_gather | solution.py:28
  9.7 102.1 %all-gather.4.cloned.1.call-start = ((), (), s32[]{:S(2)}) async-start(), calls=%async_computation.2 | async-start | bytes 4456448 | tf_op jit(solution)/shard_map/all_gather | solution.py:33
  12.0 158.6 %all-gather.8.cloned.1.call-start = ((), (), s32[]{:S(2)}) async-start(), calls=%async_computation.4 | async-start | bytes 4456448 | tf_op jit(solution)/shard_map/all_gather | solution.py:32
  14.2 595.7 %all-reduce.2.cloned.1.call-start = ((), (), s32[]{:S(2)}) async-start(), calls=%async_computation.5 | async-start | bytes 131072 | tf_op jit(solution)/shard_map/pmax | solution.py:81
  196.4 4.5 copy-start.2
  237.6 4.5 copy-start.2
  278.8 4.5 copy-start.2
  320.1 4.5 copy-start.2
  361.3 4.5 copy-start.2
  402.5 4.5 copy-start.2
  443.7 4.5 copy-start.2
  484.9 4.5 copy-start.2
  512.2 152.5 %reduce-scatter.5.cloned.1.call-start = ((), (), s32[]{:S(2)}) async-start(), calls=%async_computation.7 | async-start | bytes 69632 | tf_op jit(solution)/shard_map/reduce_scatter | solution.py:90
  611.5 116.7 %reduce-scatter.3.cloned.1.call-start = ((), (), s32[]{:S(2)}) async-start(), calls=%async_computation.6 | async-start | bytes 4456448 | tf_op jit(solution)/shard_map/reduce_scatter | solution.py:87
  621.9 108.5 %copy-start.1 = (bf16[512,512]{1,0:T(8,128)(2,1)S(1)}, bf16[512,512]{1,0:T(8,128)(2,1)}, u32[]{:S(2)}) copy-start(bf16[512,512]{1,0:T(8,128)(2,1)} %param.12) | copy-start | bytes 1572868
  621.9 107.3 %copy-start.3 = (bf16[256,512]{1,0:T(8,128)(2,1)S(1)}, bf16[256,512]{1,0:T(8,128)(2,1)}, u32[]{:S(2)}) copy-start(bf16[256,512]{1,0:T(8,128)(2,1)} %param.10) | copy-start | bytes 786436
  621.9 107.3 %copy-start.4 = (bf16[512,512]{1,0:T(8,128)(2,1)S(1)}, bf16[512,512]{1,0:T(8,128)(2,1)}, u32[]{:S(2)}) copy-start(bf16[512,512]{1,0:T(8,128)(2,1)} %param.15) | copy-start | bytes 1572868
Sparse Core Ops, SparseCore 0:
  9.8 44.1 all-gather.5
  56.4 55.3 all-gather.3
  114.3 56.2 all-gather.7
  512.3 97.5 all-reduce.1
  612.4 52.2 reduce-scatter.4
  667.1 61.0 reduce-scatter.2
where the time goes:
time: 743 us; the launch traced here: 737 us
  waiting for transfers between devices  296 us (40%)
  local copies, waits for them, and re-layouts  235 us (32%)
  matrix products  125 us (17%)
  other arithmetic  43.2 us (6%)
  blocking collectives  23.3 us (3%)
  between operations  13.5 us (2%)
    pmax x1, waiting for transfers between devices, body(): lax.pmax(group_peak.astype(jnp.bfloat16), 'col').astype(group_peak.dtype)  97.7 us
    dot_general x8, matrix products, attend(): jnp.einsum('ghqk,gkhd->gqhd', weight.astype(jnp.bfloat16), near_values, p...  69.5 us
    reduce_scatter x1, waiting for transfers between devices, body(): lax.psum_scatter(scaled.astype(jnp.bfloat16), 'col', scatter_dimension=0,...  62.8 us
    gather x8, local copies, waits for them, and re-layouts, attend(): key_tiles[tile_ids].reshape(tile_group, span, head_count, head_size)  62.6 us
    gather x8, local copies, waits for them, and re-layouts, attend(): value_tiles[tile_ids].reshape(tile_group, span, head_count, head_size)  62.5 us
    dot_general x8, matrix products, attend(): jnp.einsum('gqhd,gkhd->ghqk', query_block, near_keys, preferred_element_t...  48.3 us
    all_gather x1, waiting for transfers between devices, body(): lax.all_gather(key_rows, 'row', axis=0, tiled=True)  47.6 us
    all_gather x1, waiting for transfers between devices, body(): lax.all_gather(value_rows, 'row', axis=0, tiled=True)  37.5 us
  transfers between devices with their start and end apart: 6, of which 6 were waited for; matrix products, arithmetic and copies ran while one was open for 8% of the time, Pallas kernels for 0%

commit v1 on v0

v1 whole, which is shorter than its diff:
```python
import functools
import math

import jax
import jax.numpy as jnp
from jax import lax
from jax.experimental import pallas as pl
from jax.experimental.pallas import tpu as pltpu
from jax.sharding import PartitionSpec as P

TILE = 128
MAXT = 6
H = 8
HD = 64
D = 512
OWN = 256
PAY = OWN + 16
ROWS = 16
RING = 8
BLOCKS = ROWS * 2
SLOTS = BLOCKS * 2
VROWS = 80
ACC = D + 48
LOG2E = math.log2(math.e)
F32 = jnp.float32
BF16 = jnp.bfloat16
NEG = -1e30


def split3(x):
    hi = x.astype(BF16)
    rest = x - hi.astype(F32)
    mid = rest.astype(BF16)
    low = (rest - mid.astype(F32)).astype(BF16)
    return hi, mid, low


def source_kernel(src, wk_ref, wvt_ref, k_ref, v_ref, buf, sem):
    def fetch(b, slot):
        return pltpu.make_async_copy(src.at[b], buf.at[slot], sem.at[slot])

    row = lax.broadcasted_iota(jnp.int32, (16, TILE), 0)
    ones_rows = jnp.where(row == 0, 1.0, 0.0).astype(BF16)
    r = lax.broadcasted_iota(jnp.int32, (32, 512), 0)
    c = lax.broadcasted_iota(jnp.int32, (32, 512), 1)
    piece, head = r // 8, r % 8
    target = (head // 2) * 128 + 3 * (head % 2) + piece
    select = jnp.where((c == target) & (piece < 3), 1.0, 0.0).astype(BF16)

    col = lax.broadcasted_iota(jnp.int32, (TILE, 256), 1)
    empty = jnp.where((col == 128) | (col == 131), NEG, 0.0).astype(BF16)
    for p in range(4):
        k_ref[SLOTS, :, p * 256 : (p + 1) * 256] = empty
    v_ref[SLOTS] = jnp.zeros((H * VROWS, TILE), BF16)

    fetch(0, 0).start()

    def step(b, carry):
        slot = lax.rem(b, 2)

        @pl.when(b + 1 < BLOCKS)
        def _():
            fetch(b + 1, 1 - slot).start()

        fetch(b, slot).wait()
        x = buf[slot, 0:OWN, :].astype(F32)
        scale = lax.rsqrt(jnp.mean(x * x, axis=-1, keepdims=True) + 1e-06)
        normed = (x * scale).astype(BF16)
        keys = jnp.dot(normed, wk_ref[...], preferred_element_type=F32).astype(BF16)
        vals = lax.dot_general(
            wvt_ref[...], normed, (((1,), (1,)), ((), ())), preferred_element_type=F32
        ).astype(BF16)
        prior = buf[slot, OWN : OWN + 16, 0:OWN].astype(F32)[0:8] * LOG2E
        hi, mid, low = split3(prior)
        stack = jnp.concatenate(
            [hi.astype(F32), mid.astype(F32), low.astype(F32), jnp.zeros((8, OWN), F32)], axis=0
        ).astype(BF16)
        aux = lax.dot_general(
            stack, select, (((0,), (0,)), ((), ())), preferred_element_type=F32
        ).astype(BF16)
        for half in range(2):
            rows = slice(half * TILE, (half + 1) * TILE)
            for p in range(4):
                k_ref[2 * b + half, :, p * 256 : p * 256 + 128] = keys[rows, p * 128 : (p + 1) * 128]
                k_ref[2 * b + half, :, p * 256 + 128 : (p + 1) * 256] = aux[rows, p * 128 : (p + 1) * 128]
            for h in range(H):
                v_ref[2 * b + half, h * VROWS : h * VROWS + HD, :] = vals[h * HD : (h + 1) * HD, rows]
                v_ref[2 * b + half, h * VROWS + HD : (h + 1) * VROWS, :] = ones_rows
        return carry

    lax.fori_loop(0, BLOCKS, step, 0)


def project_source(src, w_key, w_value_t):
    return pl.pallas_call(
        source_kernel,
        out_shape=(
            pltpu.VMEM((SLOTS + 1, TILE, 1024), BF16),
            pltpu.VMEM((SLOTS + 1, H * VROWS, TILE), BF16),
        ),
        in_specs=[
            pl.BlockSpec(memory_space=pl.ANY),
            pl.BlockSpec(memory_space=pltpu.VMEM),
            pl.BlockSpec(memory_space=pltpu.VMEM),
        ],
        out_specs=(pl.BlockSpec(memory_space=pltpu.VMEM), pl.BlockSpec(memory_space=pltpu.VMEM)),
        scratch_shapes=[pltpu.VMEM((2, PAY, D), BF16), pltpu.SemaphoreType.DMA((2,))],
        compiler_params=pltpu.CompilerParams(vmem_limit_bytes=12 * 1024 * 1024),
        cost_estimate=pl.CostEstimate(
            flops=2 * BLOCKS * OWN * D * D * 2, bytes_accessed=BLOCKS * PAY * D * 2, transcendentals=0
        ),
        name="project_source",
    )(src, w_key, w_value_t)


def chunk_kernel(chunk, list_ref, pair_ref, q_ref, k_ref, v_ref, prev_ref, out_ref, rhs, s_scr, acc):
    del prev_ref
    row = lax.broadcasted_iota(jnp.int32, (TILE, 256), 0)
    col = lax.broadcasted_iota(jnp.int32, (TILE, 256), 1)
    ones = jnp.where((row < 3) & (col < 128) | (row >= 3) & (row < 6) & (col >= 128), 1.0, 0.0)
    for p in range(4):
        rhs[p, 0:HD, 128:256] = jnp.zeros((HD, 128), BF16)
        rhs[p, HD:128, 0:128] = jnp.zeros((HD, 128), BF16)
        rhs[p, 128:256, :] = ones.astype(BF16)
    for half in range(2):
        lanes = slice(half * TILE, (half + 1) * TILE)
        for p in range(4):
            rhs[p, 0:HD, 0:128] = q_ref[p * 128 : p * 128 + HD, lanes]
            rhs[p, HD:128, 128:256] = q_ref[p * 128 + HD : (p + 1) * 128, lanes]
        acc[...] = jnp.zeros(acc.shape, F32)
        pairs = pair_ref[chunk * 2 + half]
        base = (chunk * 2 + half) * 2 * MAXT

        def score(it, peaks):
            tiles = (list_ref[base + 2 * it], list_ref[base + 2 * it + 1])
            found = []
            for p in range(4):
                best = peaks[p]
                for j in range(2):
                    s = jnp.dot(
                        k_ref[tiles[j], :, p * 256 : (p + 1) * 256], rhs[p], preferred_element_type=F32
                    )
                    s_scr[it, p, j * TILE : (j + 1) * TILE, :] = s
                    best = jnp.maximum(best, jnp.max(s.reshape(16, 8, 256), axis=0))
                found.append(best)
            return tuple(found)

        peaks = lax.fori_loop(0, pairs, score, tuple(jnp.full((8, 256), -3e38, F32) for _ in range(4)))
        peaks = [jnp.max(x, axis=0, keepdims=True) for x in peaks]

        def weigh(it, carry):
            tiles = (list_ref[base + 2 * it], list_ref[base + 2 * it + 1])
            for p in range(4):
                w = jnp.exp2(s_scr[it, p] - peaks[p]).astype(BF16)
                for g in range(2):
                    h = 2 * p + g
                    rows = slice(h * VROWS, (h + 1) * VROWS)
                    v = jnp.concatenate([v_ref[tiles[0], rows, :], v_ref[tiles[1], rows, :]], axis=1)
                    acc[rows, :] += jnp.dot(v, w[:, g * 128 : (g + 1) * 128], preferred_element_type=F32)
            return carry

        lax.fori_loop(0, pairs, weigh, 0)
        for h in range(H):
            out_ref[h * HD : (h + 1) * HD, lanes] = acc[h * VROWS : h * VROWS + HD, :].astype(BF16)
        total = jnp.concatenate([acc[h * VROWS + HD : h * VROWS + HD + 1, :] for h in range(H)], axis=0)
        peak = jnp.concatenate([peaks[h // 2][:, (h % 2) * 128 : (h % 2 + 1) * 128] for h in range(H)], axis=0)
        t_hi, t_mid, _ = split3(total)
        p_hi, p_mid, p_low = split3(peak)
        pieces = [x.astype(F32) for x in (t_hi, t_mid, p_hi, p_mid, p_low)] + [jnp.zeros((8, TILE), F32)]
        out_ref[D:ACC, lanes] = jnp.concatenate(pieces, axis=0).astype(BF16)


def attend_chunk(chunk, lists, pairs, queries, keys, values, prev):
    return pl.pallas_call(
        functools.partial(chunk_kernel, chunk),
        out_shape=jax.ShapeDtypeStruct((ACC, OWN), BF16),
        in_specs=[
            pl.BlockSpec(memory_space=pltpu.SMEM),
            pl.BlockSpec(memory_space=pltpu.SMEM),
            pl.BlockSpec(memory_space=pltpu.VMEM),
            pl.BlockSpec(memory_space=pltpu.VMEM),
            pl.BlockSpec(memory_space=pltpu.VMEM),
            pl.BlockSpec(memory_space=pl.ANY),
        ],
        out_specs=pl.BlockSpec(memory_space=pltpu.VMEM),
        scratch_shapes=[
            pltpu.VMEM((4, 256, 256), BF16),
            pltpu.VMEM((MAXT, 4, 256, 256), F32),
            pltpu.VMEM((H * VROWS, TILE), F32),
        ],
        compiler_params=pltpu.CompilerParams(vmem_limit_bytes=16 * 1024 * 1024),
        cost_estimate=pl.CostEstimate(flops=4_000_000_000, bytes_accessed=1_000_000, transcendentals=0),
        name="attend_chunk",
    )(lists, pairs, queries, keys, values, prev)


def merge_kernel(*refs):
    parts, (ent_ref, w_ref, out_ref, att) = refs[:RING], refs[RING:]

    def rows(ref, i):
        return ref[D + 8 * i : D + 8 * i + 8, :].astype(F32)

    peaks, totals = [], []
    for ref in parts:
        aux = ref[D:ACC, :].astype(F32)
        totals.append(aux[0:8] + aux[8:16])
        peaks.append(aux[16:24] + aux[24:32] + aux[32:40])
    top = functools.reduce(jnp.maximum, peaks)
    factors = [jnp.exp2(x - top) for x in peaks]
    total = functools.reduce(jnp.add, [f * t for f, t in zip(factors, totals)])
    factors = [f / total for f in factors]
    for h in range(H):
        num = functools.reduce(
            jnp.add,
            [
                ref[h * HD : (h + 1) * HD, :].astype(F32) * f[h : h + 1, :]
                for ref, f in zip(parts, factors)
            ],
        )
        att[h * HD : (h + 1) * HD, :] = num.astype(BF16)
    out_ref[...] = ent_ref[...].astype(F32) + lax.dot_general(
        att[...], w_ref[...], (((0,), (0,)), ((), ())), preferred_element_type=F32
    )


def merge(parts, entities, w_out):
    return pl.pallas_call(
        merge_kernel,
        out_shape=jax.ShapeDtypeStruct((OWN, D), F32),
        in_specs=[pl.BlockSpec(memory_space=pltpu.VMEM)] * (RING + 2),
        out_specs=pl.BlockSpec(memory_space=pltpu.VMEM),
        scratch_shapes=[pltpu.VMEM((D, OWN), BF16)],
        compiler_params=pltpu.CompilerParams(vmem_limit_bytes=16 * 1024 * 1024),
        cost_estimate=pl.CostEstimate(flops=2 * OWN * D * D, bytes_accessed=3_000_000, transcendentals=0),
        name="merge",
    )(*parts, entities, w_out)


def along_z(k):
    return [(z * 2 + c, ((z + k) % RING) * 2 + c) for z in range(RING) for c in range(2)]


def across_cores():
    return [(z * 2 + c, z * 2 + 1 - c) for z in range(RING) for c in range(2)]


def neighbour_lists(tile_index, tile_count):
    me = lax.axis_index("col")
    core, z = me % 2, me // 2
    packed = jnp.concatenate([tile_index[:, 0, :], tile_count], axis=1).reshape(RING, 2, 2, MAXT + 1)
    own = lax.dynamic_index_in_dim(packed, core, 1, keepdims=False)
    other = lax.dynamic_index_in_dim(packed, 1 - core, 1, keepdims=False)
    came = lax.ppermute(other, "col", across_cores())
    first = jnp.where(core == 0, own, came)
    second = jnp.where(core == 0, came, own)

    def slots(x, group):
        t = x[..., :MAXT]
        return (t // 2 * 2 + group) * 2 + t % 2

    n0, n1 = first[..., MAXT:], second[..., MAXT:]
    pos = lax.broadcasted_iota(jnp.int32, (1, 1, 2 * MAXT), 2)
    both = jnp.concatenate([slots(first, 0), slots(second, 1)], axis=-1)
    pick = jnp.where(pos < n0, pos, MAXT + pos - n0)
    source = lax.broadcasted_iota(jnp.int32, (1, 1, 1, 2 * MAXT), 3)
    chosen = jnp.sum(jnp.where(pick[..., None] == source, both[..., None, :], 0), axis=-1)
    chosen = jnp.where(pos < n0 + n1, chosen, SLOTS)
    pairs = (n0 + n1 + 1)[..., 0] // 2
    chosen = jnp.roll(chosen, -z, axis=0)
    pairs = jnp.roll(pairs, -z, axis=0)
    return chosen.reshape(-1), pairs.reshape(-1)


def body(entities, entity_bias, w_query, w_key, w_value, w_out, tile_index, tile_count):
    payload = jnp.concatenate([entities, jnp.pad(entity_bias, ((0, 8), (0, D - OWN)))], axis=0)
    groups = [[r * 16 + z * 2 + c for r in range(ROWS) for c in range(2)] for z in range(RING)]
    source = lax.all_gather(payload, ("row", "col"), axis=0, tiled=False, axis_index_groups=groups)

    x = entities.astype(F32)
    normed = (x * lax.rsqrt(jnp.mean(x * x, axis=-1, keepdims=True) + 1e-06)).astype(BF16)
    queries = (
        lax.dot_general(w_query, normed, (((0,), (1,)), ((), ())), preferred_element_type=F32)
        * (LOG2E / math.sqrt(HD))
    ).astype(BF16)
    order = (4, 3, -3, 2, -2, 1, -1, 0)
    held = {k: lax.ppermute(queries, "col", along_z(-k)) if k else queries for k in order}
    lists, pairs = neighbour_lists(tile_index, tile_count)

    keys, values = project_source(source, w_key, w_value.T)
    prev = lists
    parts = []
    for k in order:
        prev = attend_chunk(k % RING, lists, pairs, held[k], keys, values, prev)
        parts.append(lax.ppermute(prev, "col", along_z(k)) if k else prev)
    return merge(parts, entities, w_out)


def solution(mesh):
    placed = (
        P(("row", "col"), None),
        P(None, ("row", "col")),
        P(),
        P(),
        P(),
        P(),
        P("row", "col", None),
        P("row", "col"),
    )
    return jax.shard_map(
        body, mesh=mesh, in_specs=placed, out_specs=P(("row", "col"), None), check_vma=False
    )
```

time: 743 us -> 219 us (0.29)
  waiting for transfers between devices: 296 us -> 68.6 us
  local copies, waits for them, and re-layouts: 235 us -> 19.7 us
  matrix products: 125 us -> 1.37 us
  Pallas kernels: 0 us -> 71.6 us
  other arithmetic: 43.2 us -> 5.16 us
  starting transfers between devices: 0.21 us -> 36.1 us
  blocking collectives: 23.3 us -> 0 us
    gather x24 -> x0, local copies, waits for them, and re-layouts: 130 us -> none  [the longest x8 62.6 us: attend(): key_tiles[tile_ids].reshape(tile_group, span, head_count, head_size)]
    dot_general x20 -> x1, matrix products: 125 us -> 1.37 us  [body(): lax.dot_general(w_query, normed, (((0,), (1,)), ((), ())), preferred_elem...]
    reduce_scatter x2 -> x0, waiting for transfers between devices: 99.1 us -> none  [the longest x1 62.8 us: body(): lax.psum_scatter(scaled.astype(jnp.bfloat16), 'col', scatter_dimension=0,...]
    pmax x1 -> x0, waiting for transfers between devices: 97.7 us -> none  [body(): lax.pmax(group_peak.astype(jnp.bfloat16), 'col').astype(group_peak.dtype)]
    pallas_call x0 -> x10, Pallas kernels: none -> 71.6 us  [the longest x8 50.3 us: attend_chunk(): pl.pallas_call(functools.partial(chunk_kernel, chunk), out_shape=jax.Shap...]
    all_gather x3 -> x1, waiting for transfers between devices: 98.9 us -> 40.1 us  [body(): lax.all_gather(payload, ('row', 'col'), axis=0, tiled=False, axis_index_g...]
    while x17 -> x0, local copies, waits for them, and re-layouts: 45.3 us -> none
    ppermute x0 -> x15, starting transfers between devices: none -> 36 us  [the longest x7 19.5 us: body(): parts.append(lax.ppermute(prev, 'col', along_z(k)) if k else prev)]
  transfers between devices with their start and end apart: 6 -> 16, of which waited for: 6 -> 5; matrix products, arithmetic and copies ran while one was open for 8% -> 4% of each run, Pallas kernels for 0% -> 29%
where the time goes in v1:
time: 219 us; the launch traced here: 216 us
  Pallas kernels  71.6 us (33%)
  waiting for transfers between devices  68.6 us (31%)
  starting transfers between devices  36.1 us (16%)
  local copies, waits for them, and re-layouts  19.7 us (9%)
  between operations  13.7 us (6%)
  other arithmetic  5.16 us (2%)
    pallas_call x8, Pallas kernels, attend_chunk(): pl.pallas_call(functools.partial(chunk_kernel, chunk), out_shape=jax.Shap...  50.3 us
    all_gather x1, waiting for transfers between devices, body(): lax.all_gather(payload, ('row', 'col'), axis=0, tiled=False, axis_index_g...  40.1 us
    ppermute x7, waiting for transfers between devices, body(): parts.append(lax.ppermute(prev, 'col', along_z(k)) if k else prev)  28.4 us
    pallas_call x1, Pallas kernels, project_source(): pl.pallas_call(source_kernel, out_shape=(pltpu.VMEM((SLOTS + 1, TILE, 102...  19.8 us
    ppermute x7, starting transfers between devices, body(): parts.append(lax.ppermute(prev, 'col', along_z(k)) if k else prev)  19.5 us
    unnamed x17, local copies, waits for them, and re-layouts  18.9 us
    ppermute x7, starting transfers between devices, body(): lax.ppermute(queries, 'col', along_z(-k))  16.5 us
  transfers between devices with their start and end apart: 16, of which 5 were waited for; matrix products, arithmetic and copies ran while one was open for 4% of the time, Pallas kernels for 29%

profile of v1, /device:TPU:56, one launch (start us, length us, event | category | flops | bytes accessed | tf_op | source)
XLA Modules:
  0.0 216.2 jit_solution(365412599461090760)
XLA Ops:
  10.8 6.4 %collective-permute-start.1 = (bf16[512,256]{1,0:T(8,128)(2,1)S(1)}, bf16[512,256]{1,0:T(8,128)(2,1)S(1)}, u32[]{:S(2)}, u32[]{:S(2)}) collective-permute-start(bf16[512,256]{1,0:T(8,128)(2,1)S(1)} %fusion.1.q_ref), channel_id=1, source_target_pairs={{0,8},{1,9},{2,10},{3,11},{4,12},{5,13},{6,14},{7,15},{8,0},{9,1},... | collective-permute-start | bytes 786440 | tf_op jit(solution)/shard_map/ppermute | solution.py:286
  17.3 4.9 %collective-permute-start.5 = (bf16[512,256]{1,0:T(8,128)(2,1)S(1)}, bf16[512,256]{1,0:T(8,128)(2,1)S(1)}, u32[]{:S(2)}, u32[]{:S(2)}) collective-permute-start(bf16[512,256]{1,0:T(8,128)(2,1)S(1)} %fusion.1.q_ref), channel_id=1, source_target_pairs={{0,6},{1,7},{2,8},{3,9},{4,10},{5,11},{6,12},{7,13},{8,14},{9,15},... | collective-permute-start | bytes 786440 | tf_op jit(solution)/shard_map/ppermute | solution.py:286
  27.2 2.4 %collective-permute-start.9 = (bf16[512,256]{1,0:T(8,128)(2,1)S(1)}, bf16[512,256]{1,0:T(8,128)(2,1)S(1)}, u32[]{:S(2)}, u32[]{:S(2)}) collective-permute-start(bf16[512,256]{1,0:T(8,128)(2,1)S(1)} %fusion.1.q_ref), channel_id=1, source_target_pairs={{0,4},{1,5},{2,6},{3,7},{4,8},{5,9},{6,10},{7,11},{8,12},{9,13},{1... | collective-permute-start | bytes 786440 | tf_op jit(solution)/shard_map/ppermute | solution.py:286
  31.1 40.1 %all-gather.3.cloned.1.call-done = bf16[8704,512]{1,0:T(8,128)(2,1)} async-done(((bf16[272,512]{1,0:T(8,128)(2,1)}), bf16[8704,512]{1,0:T(8,128)(2,1)}) %all-gather.3.cloned.1.call-update) | async-done | bytes 8912912 | tf_op jit(solution)/shard_map/all_gather | solution.py:277
  71.2 3.5 %copy-done.5 = bf16[8704,512]{1,0:T(8,128)(2,1)S(1)} copy-done((bf16[8704,512]{1,0:T(8,128)(2,1)S(1)}, bf16[8704,512]{1,0:T(8,128)(2,1)}, u32[]{:S(2)}) %copy-start.5) | copy-done | bytes 8912920
  75.8 19.8 %project_source.1 = (bf16[65,128,1024]{2,1,0:T(8,128)(2,1)S(1)}, bf16[65,640,128]{2,1,0:T(8,128)(2,1)S(1)}) custom-call(bf16[32,272,512]{2,1,0:T(8,128)(2,1)S(1)} %bitcast.24, bf16[512,512]{1,0:T(8,128)(2,1)S(1)} %copy-done.6, bf16[512,512]{1,0:T(8,128)(2,1)S(1)} %bitcast.23), custom_call_target="tpu_custom_call" | custom-call | flops 8589934592 | bytes 8912896 | tf_op jit(solution)/shard_map/project_source/pallas_call | solution.py:95
  95.6 5.8 %copy-done.1 = bf16[65,128,1024]{2,1,0:T(8,128)(2,1)} copy-done((bf16[65,128,1024]{2,1,0:T(8,128)(2,1)}, bf16[65,128,1024]{2,1,0:T(8,128)(2,1)S(1)}, u32[]{:S(2)}) %copy-start.1) | copy-done | bytes 17039384
  101.9 5.8 %copy-done.2 = bf16[65,128,1024]{2,1,0:T(8,128)(2,1)S(1)} copy-done((bf16[65,128,1024]{2,1,0:T(8,128)(2,1)S(1)}, bf16[65,128,1024]{2,1,0:T(8,128)(2,1)}, u32[]{:S(2)}) %copy-start.2) | copy-done | bytes 17039384
  107.8 6.5 %attend_chunk.8.prev_ref = bf16[560,256]{1,0:T(8,128)(2,1)S(1)} custom-call(s32[192]{0:T(256)S(1)} %reshape.31.list_ref.prev_ref, s32[16]{0:T(128)S(1)} %reshape.32.pair_ref, bf16[512,256]{1,0:T(8,128)(2,1)S(1)} %collective-permute-done.1.q_ref, bf16[65,128,1024]{2,1,0:T(8,128)(2,1)S(1)} %copy-done.2, bf16[65,640,128]{2,1,0:T(8,128)(2,1)S(1)} %get-tuple-element.8.v_ref, ...), custom_call_target="tpu_custom_call" | custom-call | flops 4000000000 | bytes 1000000 | tf_op jit(solution)/shard_map/attend_chunk/pallas_call | solution.py:174
  115.9 6.5 %attend_chunk.9.prev_ref = bf16[560,256]{1,0:T(8,128)(2,1)S(1)} custom-call(s32[192]{0:T(256)S(1)} %reshape.31.list_ref.prev_ref, s32[16]{0:T(128)S(1)} %reshape.32.pair_ref, bf16[512,256]{1,0:T(8,128)(2,1)S(1)} %collective-permute-done.3.q_ref, bf16[65,128,1024]{2,1,0:T(8,128)(2,1)S(1)} %copy-done.2, bf16[65,640,128]{2,1,0:T(8,128)(2,1)S(1)} %get-tuple-element.8.v_ref, ...), custom_call_target="tpu_custom_call" | custom-call | flops 4000000000 | bytes 1000000 | tf_op jit(solution)/shard_map/attend_chunk/pallas_call | solution.py:174
  122.4 5.9 %attend_chunk.10.prev_ref = bf16[560,256]{1,0:T(8,128)(2,1)S(1)} custom-call(s32[192]{0:T(256)S(1)} %reshape.31.list_ref.prev_ref, s32[16]{0:T(128)S(1)} %reshape.32.pair_ref, bf16[512,256]{1,0:T(8,128)(2,1)S(1)} %collective-permute-done.5.q_ref, bf16[65,128,1024]{2,1,0:T(8,128)(2,1)S(1)} %copy-done.2, bf16[65,640,128]{2,1,0:T(8,128)(2,1)S(1)} %get-tuple-element.8.v_ref, ...), custom_call_target="tpu_custom_call" | custom-call | flops 4000000000 | bytes 1000000 | tf_op jit(solution)/shard_map/attend_chunk/pallas_call | solution.py:174
  128.3 5.4 %attend_chunk.11.prev_ref = bf16[560,256]{1,0:T(8,128)(2,1)S(1)} custom-call(s32[192]{0:T(256)S(1)} %reshape.31.list_ref.prev_ref, s32[16]{0:T(128)S(1)} %reshape.32.pair_ref, bf16[512,256]{1,0:T(8,128)(2,1)S(1)} %collective-permute-done.7.q_ref, bf16[65,128,1024]{2,1,0:T(8,128)(2,1)S(1)} %copy-done.2, bf16[65,640,128]{2,1,0:T(8,128)(2,1)S(1)} %get-tuple-element.8.v_ref, ...), custom_call_target="tpu_custom_call" | custom-call | flops 4000000000 | bytes 1000000 | tf_op jit(solution)/shard_map/attend_chunk/pallas_call | solution.py:174
  133.7 6.5 %attend_chunk.12.prev_ref = bf16[560,256]{1,0:T(8,128)(2,1)S(1)} custom-call(s32[192]{0:T(256)S(1)} %reshape.31.list_ref.prev_ref, s32[16]{0:T(128)S(1)} %reshape.32.pair_ref, bf16[512,256]{1,0:T(8,128)(2,1)S(1)} %collective-permute-done.9.q_ref, bf16[65,128,1024]{2,1,0:T(8,128)(2,1)S(1)} %copy-done.2, bf16[65,640,128]{2,1,0:T(8,128)(2,1)S(1)} %get-tuple-element.8.v_ref, ...), custom_call_target="tpu_custom_call" | custom-call | flops 4000000000 | bytes 1000000 | tf_op jit(solution)/shard_map/attend_chunk/pallas_call | solution.py:174
  140.3 6.5 %attend_chunk.13.prev_ref = bf16[560,256]{1,0:T(8,128)(2,1)S(1)} custom-call(s32[192]{0:T(256)S(1)} %reshape.31.list_ref.prev_ref, s32[16]{0:T(128)S(1)} %reshape.32.pair_ref, bf16[512,256]{1,0:T(8,128)(2,1)S(1)} %collective-permute-done.11.q_ref, bf16[65,128,1024]{2,1,0:T(8,128)(2,1)S(1)} %copy-done.2, bf16[65,640,128]{2,1,0:T(8,128)(2,1)S(1)} %get-tuple-element.8.v_ref, ...), custom_call_target="tpu_custom_call" | custom-call | flops 4000000000 | bytes 1000000 | tf_op jit(solution)/shard_map/attend_chunk/pallas_call | solution.py:174
  146.8 7.1 %attend_chunk.14.prev_ref = bf16[560,256]{1,0:T(8,128)(2,1)S(1)} custom-call(s32[192]{0:T(256)S(1)} %reshape.31.list_ref.prev_ref, s32[16]{0:T(128)S(1)} %reshape.32.pair_ref, bf16[512,256]{1,0:T(8,128)(2,1)S(1)} %collective-permute-done.13.q_ref, bf16[65,128,1024]{2,1,0:T(8,128)(2,1)S(1)} %copy-done.2, bf16[65,640,128]{2,1,0:T(8,128)(2,1)S(1)} %get-tuple-element.8.v_ref, ...), custom_call_target="tpu_custom_call" | custom-call | flops 4000000000 | bytes 1000000 | tf_op jit(solution)/shard_map/attend_chunk/pallas_call | solution.py:174
  154.0 2.0 collective-permute-start.12
  156.0 2.9 %collective-permute-start.8 = (bf16[560,256]{1,0:T(8,128)(2,1)S(1)}, bf16[560,256]{1,0:T(8,128)(2,1)S(1)}, u32[]{:S(2)}, u32[]{:S(2)}) collective-permute-start(bf16[560,256]{1,0:T(8,128)(2,1)S(1)} %attend_chunk.11.prev_ref), channel_id=1, source_target_pairs={{0,4},{1,5},{2,6},{3,7},{4,8},{5,9},{6,10},{7,11},{8,12},{9,13},{1... | collective-permute-start | bytes 860168 | tf_op jit(solution)/shard_map/ppermute | solution.py:294
  159.0 4.0 %collective-permute-start.6 = (bf16[560,256]{1,0:T(8,128)(2,1)S(1)}, bf16[560,256]{1,0:T(8,128)(2,1)S(1)}, u32[]{:S(2)}, u32[]{:S(2)}) collective-permute-start(bf16[560,256]{1,0:T(8,128)(2,1)S(1)} %attend_chunk.10.prev_ref), channel_id=1, source_target_pairs={{0,10},{1,11},{2,12},{3,13},{4,14},{5,15},{6,0},{7,1},{8,2},{9,3},... | collective-permute-start | bytes 860168 | tf_op jit(solution)/shard_map/ppermute | solution.py:294
  163.0 2.0 collective-permute-done.14.refs_6_
  164.9 3.7 %collective-permute-start.4 = (bf16[560,256]{1,0:T(8,128)(2,1)S(1)}, bf16[560,256]{1,0:T(8,128)(2,1)S(1)}, u32[]{:S(2)}, u32[]{:S(2)}) collective-permute-start(bf16[560,256]{1,0:T(8,128)(2,1)S(1)} %attend_chunk.9.prev_ref), channel_id=1, source_target_pairs={{0,6},{1,7},{2,8},{3,9},{4,10},{5,11},{6,12},{7,13},{8,14},{9,15},... | collective-permute-start | bytes 860168 | tf_op jit(solution)/shard_map/ppermute | solution.py:294
  168.6 6.8 %collective-permute-start.2 = (bf16[560,256]{1,0:T(8,128)(2,1)S(1)}, bf16[560,256]{1,0:T(8,128)(2,1)S(1)}, u32[]{:S(2)}, u32[]{:S(2)}) collective-permute-start(bf16[560,256]{1,0:T(8,128)(2,1)S(1)} %attend_chunk.8.prev_ref), channel_id=1, source_target_pairs={{0,8},{1,9},{2,10},{3,11},{4,12},{5,13},{6,14},{7,15},{8,0},{9,1},... | collective-permute-start | bytes 860168 | tf_op jit(solution)/shard_map/ppermute | solution.py:294
  175.4 5.9 %attend_chunk.15.refs_7_ = bf16[560,256]{1,0:T(8,128)(2,1)S(1)} custom-call(s32[192]{0:T(256)S(1)} %reshape.31.list_ref.prev_ref, s32[16]{0:T(128)S(1)} %reshape.32.pair_ref, bf16[512,256]{1,0:T(8,128)(2,1)S(1)} %fusion.1.q_ref, bf16[65,128,1024]{2,1,0:T(8,128)(2,1)S(1)} %copy-done.2, bf16[65,640,128]{2,1,0:T(8,128)(2,1)S(1)} %get-tuple-element.8.v_ref, ...), custom_call_target="tpu_custom_call" | custom-call | flops 4000000000 | bytes 1000000 | tf_op jit(solution)/shard_map/attend_chunk/pallas_call | solution.py:174
  181.3 10.9 %collective-permute-done.6.refs_2_ = bf16[560,256]{1,0:T(8,128)(2,1)S(1)} collective-permute-done((bf16[560,256]{1,0:T(8,128)(2,1)S(1)}, bf16[560,256]{1,0:T(8,128)(2,1)S(1)}, u32[]{:S(2)}, u32[]{:S(2)}) %collective-permute-start.6) | collective-permute-done | bytes 286752 | tf_op jit(solution)/shard_map/ppermute | solution.py:294
  192.3 13.8 %collective-permute-done.4.refs_1_ = bf16[560,256]{1,0:T(8,128)(2,1)S(1)} collective-permute-done((bf16[560,256]{1,0:T(8,128)(2,1)S(1)}, bf16[560,256]{1,0:T(8,128)(2,1)S(1)}, u32[]{:S(2)}, u32[]{:S(2)}) %collective-permute-start.4) | collective-permute-done | bytes 286752 | tf_op jit(solution)/shard_map/ppermute | solution.py:294
  (62 shorter events, 17.2 us)
Async XLA Ops:
  6.5 2.9 %copy-start = (bf16[512,512]{1,0:T(8,128)(2,1)S(1)}, bf16[512,512]{1,0:T(8,128)(2,1)}, u32[]{:S(2)}) copy-start(bf16[512,512]{1,0:T(8,128)(2,1)} %param.10) | copy-start | bytes 1572868
  6.5 64.7 %all-gather.3.cloned.1.call-start = ((), (), s32[]{:S(2)}) async-start(), calls=%async_computation | async-start | bytes 9191424 | tf_op jit(solution)/shard_map/all_gather | solution.py:277
  10.8 90.7 %collective-permute-start.1 = (bf16[512,256]{1,0:T(8,128)(2,1)S(1)}, bf16[512,256]{1,0:T(8,128)(2,1)S(1)}, u32[]{:S(2)}, u32[]{:S(2)}) collective-permute-start(bf16[512,256]{1,0:T(8,128)(2,1)S(1)} %fusion.1.q_ref), channel_id=1, source_target_pairs={{0,8},{1,9},{2,10},{3,11},{4,12},{5,13},{6,14},{7,15},{8,0},{9,1},... | collective-permute-start | bytes 786440 | tf_op jit(solution)/shard_map/ppermute | solution.py:286
  17.2 97.1 %collective-permute-start.3 = (bf16[512,256]{1,0:T(8,128)(2,1)S(1)}, bf16[512,256]{1,0:T(8,128)(2,1)S(1)}, u32[]{:S(2)}, u32[]{:S(2)}) collective-permute-start(bf16[512,256]{1,0:T(8,128)(2,1)S(1)} %fusion.1.q_ref), channel_id=1, source_target_pairs={{0,10},{1,11},{2,12},{3,13},{4,14},{5,15},{6,0},{7,1},{8,2},{9,3},... | collective-permute-start | bytes 786440 | tf_op jit(solution)/shard_map/ppermute | solution.py:286
  17.3 105.1 %collective-permute-start.5 = (bf16[512,256]{1,0:T(8,128)(2,1)S(1)}, bf16[512,256]{1,0:T(8,128)(2,1)S(1)}, u32[]{:S(2)}, u32[]{:S(2)}) collective-permute-start(bf16[512,256]{1,0:T(8,128)(2,1)S(1)} %fusion.1.q_ref), channel_id=1, source_target_pairs={{0,6},{1,7},{2,8},{3,9},{4,10},{5,11},{6,12},{7,13},{8,14},{9,15},... | collective-permute-start | bytes 786440 | tf_op jit(solution)/shard_map/ppermute | solution.py:286
  22.2 106.1 %collective-permute-start.7 = (bf16[512,256]{1,0:T(8,128)(2,1)S(1)}, bf16[512,256]{1,0:T(8,128)(2,1)S(1)}, u32[]{:S(2)}, u32[]{:S(2)}) collective-permute-start(bf16[512,256]{1,0:T(8,128)(2,1)S(1)} %fusion.1.q_ref), channel_id=1, source_target_pairs={{0,12},{1,13},{2,14},{3,15},{4,0},{5,1},{6,2},{7,3},{8,4},{9,5},{1... | collective-permute-start | bytes 786440 | tf_op jit(solution)/shard_map/ppermute | solution.py:286
  25.8 1.4 collective-permute-start
  27.2 106.5 %collective-permute-start.9 = (bf16[512,256]{1,0:T(8,128)(2,1)S(1)}, bf16[512,256]{1,0:T(8,128)(2,1)S(1)}, u32[]{:S(2)}, u32[]{:S(2)}) collective-permute-start(bf16[512,256]{1,0:T(8,128)(2,1)S(1)} %fusion.1.q_ref), channel_id=1, source_target_pairs={{0,4},{1,5},{2,6},{3,7},{4,8},{5,9},{6,10},{7,11},{8,12},{9,13},{1... | collective-permute-start | bytes 786440 | tf_op jit(solution)/shard_map/ppermute | solution.py:286
  71.2 3.5 %copy-start.5 = (bf16[8704,512]{1,0:T(8,128)(2,1)S(1)}, bf16[8704,512]{1,0:T(8,128)(2,1)}, u32[]{:S(2)}) copy-start(bf16[8704,512]{1,0:T(8,128)(2,1)} %all-gather.3.cloned.1.call-done) | copy-start | bytes 26738692
  74.7 1.0 copy-start.6
  95.6 5.8 %copy-start.1 = (bf16[65,128,1024]{2,1,0:T(8,128)(2,1)}, bf16[65,128,1024]{2,1,0:T(8,128)(2,1)S(1)}, u32[]{:S(2)}) copy-start(bf16[65,128,1024]{2,1,0:T(8,128)(2,1)S(1)} %get-tuple-element.7.k_ref) | copy-start | bytes 51118084
  101.5 38.8 %collective-permute-start.11 = (bf16[512,256]{1,0:T(8,128)(2,1)S(1)}, bf16[512,256]{1,0:T(8,128)(2,1)S(1)}, u32[]{:S(2)}, u32[]{:S(2)}) collective-permute-start(bf16[512,256]{1,0:T(8,128)(2,1)S(1)} %fusion.1.q_ref), channel_id=1, source_target_pairs={{0,14},{1,15},{2,0},{3,1},{4,2},{5,3},{6,4},{7,5},{8,6},{9,7},{10,... | collective-permute-start | bytes 786440 | tf_op jit(solution)/shard_map/ppermute | solution.py:286
  101.9 5.8 %copy-start.2 = (bf16[65,128,1024]{2,1,0:T(8,128)(2,1)S(1)}, bf16[65,128,1024]{2,1,0:T(8,128)(2,1)}, u32[]{:S(2)}) copy-start(bf16[65,128,1024]{2,1,0:T(8,128)(2,1)} %copy-done.1) | copy-start | bytes 51118084
  114.3 32.5 %collective-permute-start.13 = (bf16[512,256]{1,0:T(8,128)(2,1)S(1)}, bf16[512,256]{1,0:T(8,128)(2,1)S(1)}, u32[]{:S(2)}, u32[]{:S(2)}) collective-permute-start(bf16[512,256]{1,0:T(8,128)(2,1)S(1)} %fusion.1.q_ref), channel_id=1, source_target_pairs={{0,2},{1,3},{2,4},{3,5},{4,6},{5,7},{6,8},{7,9},{8,10},{9,11},{10,... | collective-permute-start | bytes 786440 | tf_op jit(solution)/shard_map/ppermute | solution.py:286
  153.9 53.9 %copy-start.3 = (bf16[256,512]{1,0:T(8,128)(2,1)S(1)}, bf16[256,512]{1,0:T(8,128)(2,1)}, u32[]{:S(2)}) copy-start(bf16[256,512]{1,0:T(8,128)(2,1)} %refs_8_.1) | copy-start | bytes 786436
  153.9 53.9 %copy-start.4 = (bf16[512,512]{1,0:T(8,128)(2,1)S(1)}, bf16[512,512]{1,0:T(8,128)(2,1)}, u32[]{:S(2)}) copy-start(bf16[512,512]{1,0:T(8,128)(2,1)} %refs_9_.1) | copy-start | bytes 1572868
  153.9 11.0 %collective-permute-start.14 = (bf16[560,256]{1,0:T(8,128)(2,1)S(1)}, bf16[560,256]{1,0:T(8,128)(2,1)S(1)}, u32[]{:S(2)}, u32[]{:S(2)}) collective-permute-start(bf16[560,256]{1,0:T(8,128)(2,1)S(1)} %attend_chunk.14.prev_ref), channel_id=1, source_target_pairs={{0,14},{1,15},{2,0},{3,1},{4,2},{5,3},{6,4},{7,5},{8,6},{9,7},{10,... | collective-permute-start | bytes 860168 | tf_op jit(solution)/shard_map/ppermute | solution.py:294
  154.0 14.6 %collective-permute-start.12 = (bf16[560,256]{1,0:T(8,128)(2,1)S(1)}, bf16[560,256]{1,0:T(8,128)(2,1)S(1)}, u32[]{:S(2)}, u32[]{:S(2)}) collective-permute-start(bf16[560,256]{1,0:T(8,128)(2,1)S(1)} %attend_chunk.13.prev_ref), channel_id=1, source_target_pairs={{0,2},{1,3},{2,4},{3,5},{4,6},{5,7},{6,8},{7,9},{8,10},{9,11},{10,... | collective-permute-start | bytes 860168 | tf_op jit(solution)/shard_map/ppermute | solution.py:294
  156.0 25.3 %collective-permute-start.10 = (bf16[560,256]{1,0:T(8,128)(2,1)S(1)}, bf16[560,256]{1,0:T(8,128)(2,1)S(1)}, u32[]{:S(2)}, u32[]{:S(2)}) collective-permute-start(bf16[560,256]{1,0:T(8,128)(2,1)S(1)} %attend_chunk.12.prev_ref), channel_id=1, source_target_pairs={{0,12},{1,13},{2,14},{3,15},{4,0},{5,1},{6,2},{7,3},{8,4},{9,5},{1... | collective-permute-start | bytes 860168 | tf_op jit(solution)/shard_map/ppermute | solution.py:294
  156.0 25.3 %collective-permute-start.8 = (bf16[560,256]{1,0:T(8,128)(2,1)S(1)}, bf16[560,256]{1,0:T(8,128)(2,1)S(1)}, u32[]{:S(2)}, u32[]{:S(2)}) collective-permute-start(bf16[560,256]{1,0:T(8,128)(2,1)S(1)} %attend_chunk.11.prev_ref), channel_id=1, source_target_pairs={{0,4},{1,5},{2,6},{3,7},{4,8},{5,9},{6,10},{7,11},{8,12},{9,13},{1... | collective-permute-start | bytes 860168 | tf_op jit(solution)/shard_map/ppermute | solution.py:294
  159.0 33.3 %collective-permute-start.6 = (bf16[560,256]{1,0:T(8,128)(2,1)S(1)}, bf16[560,256]{1,0:T(8,128)(2,1)S(1)}, u32[]{:S(2)}, u32[]{:S(2)}) collective-permute-start(bf16[560,256]{1,0:T(8,128)(2,1)S(1)} %attend_chunk.10.prev_ref), channel_id=1, source_target_pairs={{0,10},{1,11},{2,12},{3,13},{4,14},{5,15},{6,0},{7,1},{8,2},{9,3},... | collective-permute-start | bytes 860168 | tf_op jit(solution)/shard_map/ppermute | solution.py:294
  164.9 41.1 %collective-permute-start.4 = (bf16[560,256]{1,0:T(8,128)(2,1)S(1)}, bf16[560,256]{1,0:T(8,128)(2,1)S(1)}, u32[]{:S(2)}, u32[]{:S(2)}) collective-permute-start(bf16[560,256]{1,0:T(8,128)(2,1)S(1)} %attend_chunk.9.prev_ref), channel_id=1, source_target_pairs={{0,6},{1,7},{2,8},{3,9},{4,10},{5,11},{6,12},{7,13},{8,14},{9,15},... | collective-permute-start | bytes 860168 | tf_op jit(solution)/shard_map/ppermute | solution.py:294
  168.6 39.1 %collective-permute-start.2 = (bf16[560,256]{1,0:T(8,128)(2,1)S(1)}, bf16[560,256]{1,0:T(8,128)(2,1)S(1)}, u32[]{:S(2)}, u32[]{:S(2)}) collective-permute-start(bf16[560,256]{1,0:T(8,128)(2,1)S(1)} %attend_chunk.8.prev_ref), channel_id=1, source_target_pairs={{0,8},{1,9},{2,10},{3,11},{4,12},{5,13},{6,14},{7,15},{8,0},{9,1},... | collective-permute-start | bytes 860168 | tf_op jit(solution)/shard_map/ppermute | solution.py:294
Sparse Core Ops, SparseCore 0:
  9.9 61.2 all-gather.2
